TPU v7x, 256 devices: a whole 4x4x8 slice. The times are simulated.
256 devices in a mesh: patch: 64 (over z_hi, y, x), head: 4 (over z_lo, core).
Axes of the slice: x: 4, y: 4, z: 8 (z_hi: 4, z_lo: 2; z = z_hi * 2 + z_lo), core: 2. Of those that a mesh axis runs over, the one named last changes fastest.
Arguments:
- fresh_qkv: bfloat16 [2, 8192, 3, 1536], P(None, ('patch', 'head'))
- stale_kv: bfloat16 [8192, 2, 1536], P('patch', None, 'head'), may hold values from -8 to 8
- text_mask: int32 [256], replicated, may hold values 0 or 1
- out_weight: bfloat16 [1536, 3072], P('head'), may hold values from -0.15625 to 0.15625
- inputs: bfloat16 [2, 8192, 3072], P(None, ('patch', 'head')), may hold values from -6 to 6
- gate: float32 [2, 3072], replicated, may hold values from -4 to 4
Outputs:
- blended: bfloat16 [2, 8192, 3072], P(None, ('patch', 'head'))
All inputs are finite; a program needn't handle non-finite values.
Results may differ from a plain program's by a relative error of at most 0.014.
Values may be sent and summed in bfloat16 or wider, within the bound.
A program may use at most 128 MiB of HBM per device.

v0:
```python
import jax
import jax.numpy as jnp
from jax import lax
from jax.sharding import PartitionSpec as P

HEAD_DIM = 128


big_negative = -1e30


def absorb(running, queries, key_rows, value_rows, usable, score_scale):
    row_best, row_total, summed = running
    scores = (
        jnp.einsum("qhd,khd->hqk", queries, key_rows, preferred_element_type=jnp.float32)
        * score_scale
    )
    scores = jnp.where(usable[None, None, :], scores, big_negative)
    new_best = jnp.maximum(row_best, jnp.max(scores, axis=2))
    exps = jnp.where(usable[None, None, :], jnp.exp(scores - new_best[:, :, None]), 0.0)
    factor = jnp.exp(row_best - new_best)
    row_total = row_total * factor + jnp.sum(exps, axis=2)
    product = jnp.einsum(
        "hqk,khd->qhd", exps.astype(jnp.bfloat16), value_rows, preferred_element_type=jnp.float32
    )
    summed = summed * jnp.transpose(factor)[:, :, None] + product
    return (new_best, row_total, summed)


def shards(fresh_qkv, stale_kv, text_mask, out_weight, inputs, gate):
    groups = lax.axis_size("head")
    patches = lax.axis_size("patch")
    own_patch = lax.axis_index("patch")
    steps_here = fresh_qkv.shape[0]
    tok_dev = fresh_qkv.shape[1]
    patch_tok = tok_dev * groups
    local_width = fresh_qkv.shape[3] // groups
    local_heads = local_width // HEAD_DIM
    all_tokens = patch_tok * patches
    score_scale = HEAD_DIM ** (-0.5)
    valid_all = (
        jnp.concatenate([jnp.ones((all_tokens - text_mask.shape[0],), jnp.int32), text_mask]) == 1
    )
    own_first = own_patch * patch_tok
    fresh_valid = lax.dynamic_slice_in_dim(valid_all, own_first, patch_tok, 0)
    step_groups = [
        lax.all_to_all(fresh_qkv[index], "head", split_axis=2, concat_axis=0, tiled=True)
        for index in range(steps_here)
    ]
    stale_now = stale_kv
    results = []
    for step_index in range(steps_here):
        grouped = step_groups[step_index]
        queries = grouped[:, 0].reshape(patch_tok, local_heads, HEAD_DIM)
        running = (
            jnp.full((local_heads, patch_tok), big_negative, jnp.float32),
            jnp.zeros((local_heads, patch_tok), jnp.float32),
            jnp.zeros((patch_tok, local_heads, HEAD_DIM), jnp.float32),
        )
        running = absorb(
            running,
            queries,
            grouped[:, 1].reshape(patch_tok, local_heads, HEAD_DIM),
            grouped[:, 2].reshape(patch_tok, local_heads, HEAD_DIM),
            fresh_valid,
            score_scale,
        )
        gathered = lax.all_gather(stale_now, "patch", axis=0, tiled=True)
        count = gathered.shape[0]
        positions = jnp.arange(count, dtype=jnp.int32)
        usable = valid_all
        usable = usable & ((positions < own_first) | (positions >= own_first + patch_tok))
        running = absorb(
            running,
            queries,
            gathered[:, 0].reshape(count, local_heads, HEAD_DIM),
            gathered[:, 1].reshape(count, local_heads, HEAD_DIM),
            usable,
            score_scale,
        )
        row_best, row_total, summed = running
        attended = (summed / jnp.transpose(row_total)[:, :, None]).astype(jnp.bfloat16)
        attended = attended.reshape(patch_tok, local_width)
        branch = lax.psum_scatter(
            jnp.dot(attended, out_weight, preferred_element_type=jnp.float32).astype(jnp.bfloat16),
            "head",
            scatter_dimension=0,
            tiled=True,
        ).astype(jnp.float32)
        blended = inputs[step_index].astype(jnp.float32) + gate[step_index][None, :] * branch
        results.append(blended.astype(jnp.bfloat16))
        stale_now = grouped[:, 1:3]
    return jnp.stack(results)


def solution(mesh):
    placed = (
        P(None, ("patch", "head"), None, None),
        P("patch", None, "head"),
        P(),
        P("head", None),
        P(None, ("patch", "head"), None),
        P(),
    )
    return jax.shard_map(
        shards,
        mesh=mesh,
        in_specs=placed,
        out_specs=P(None, ("patch", "head"), None),
        check_vma=False,
    )
```

profile of v0, /device:TPU:1, one launch (start us, length us, event | category | flops | bytes accessed | tf_op | source)
XLA Modules:
  0.0 439.8 jit_solution(10376001261518584627)
XLA Ops:
  11.8 2.6 bitcast_bitcast_fusion.1
  14.4 2.9 reshape.38
  17.3 11.4 %all_to_all.36 = bf16[4,2,18432]{2,1,0:T(2,128)(2,1)S(1)} all-to-all(bf16[4,2,18432]{2,1,0:T(2,128)(2,1)S(1)} %reshape.38), channel_id=1, replica_groups=mesh['patch'=64,'head'=4] {'head'}, dimensions={0} | all-to-all | bytes 589824 | tf_op jit(solution)/shard_map/all_to_all | solution.py:47
  28.8 2.2 reshape.39
  31.0 2.6 copy.54
  36.5 2.6 bitcast_bitcast_fusion
  39.1 3.9 reshape.40
  43.0 4.0 all-to-all-start.1
  47.5 5.0 %all-to-all-done.1 = bf16[4,2,18432]{2,1,0:T(2,128)(2,1)S(1)} async-done(((bf16[4,2,18432]{2,1,0:T(2,128)(2,1)}), bf16[4,2,18432]{2,1,0:T(2,128)(2,1)S(1)}, u32[]{:S(2)}, u32[]{:S(2)}) %all-to-all-start.1) | async-done | bytes 294944 | tf_op jit(solution)/shard_map/all_to_all | solution.py:47
  52.5 2.2 reshape.41
  54.8 2.6 copy.66
  58.3 147.2 %all-gather.3.cloned.1.call-done = bf16[8192,2,384]{0,2,1:T(8,128)(2,1)} async-done(((bf16[128,2,384]{0,2,1:T(8,128)(2,1)}), bf16[8192,2,384]{0,2,1:T(8,128)(2,1)}) %all-gather.3.cloned.1.call-update) | async-done | bytes 12582928 | tf_op jit(solution)/shard_map/all_gather | solution.py:68
  205.5 8.3 %fusion.66 = (bf16[8192,1,384]{0,2,1:T(8,128)(2,1)}, bf16[8192,1,384]{0,2,1:T(8,128)(2,1)S(1)}) fusion(bf16[8192,2,384]{0,2,1:T(8,128)(2,1)} %all-gather.3.cloned.1.call-done), kind=kLoop, calls=%fused_computation.84 | loop fusion | bytes 25165824 | tf_op jit(solution)/shard_map/slice | solution.py:77
  213.8 7.0 %fusion.73 = (f32[3,128]{1,0:T(4,128)S(1)}, f32[3,128,8192]{2,1,0:T(8,128)}) fusion(bf16[128,3,128]{0,2,1:T(8,128)(2,1)S(1)} %bitcast.142, bf16[8192,3,128]{0,2,1:T(8,128)(2,1)S(1)} %bitcast.131, pred[8192]{0:T(1024)(128)(4,1)S(1)} %get-tuple-element.36), kind=kOutput, calls=%fused_computation.91 | convolution fusion | flops 814743168 | bytes 18982400 | tf_op jit(solution)/shard_map/qhd,khd->hqk/dot_general | solution.py:15
  220.8 8.5 %fusion.24 = f32[128,3,128]{0,2,1:T(8,128)S(1)} fusion(bf16[8192,3,128]{0,2,1:T(8,128)(2,1)} %bitcast.135, f32[3,128,8192]{2,1,0:T(8,128)} %get-tuple-element.40, f32[3,128]{1,0:T(4,128)S(1)} %get-tuple-element.34, pred[8192]{0:T(1024)(128)(4,1)S(1)} %get-tuple-element.36), kind=kOutput, calls=%fused_computation.32 | convolution fusion | flops 814743552 | bytes 19080704 | tf_op jit(solution)/shard_map/hqk,khd->qhd/dot_general | solution.py:23
  229.3 114.2 %all-gather.5.cloned.1.call-done = bf16[8192,2,384]{2,0,1:T(8,128)(2,1)} async-done(((bf16[128,2,384]{2,0,1:T(8,128)(2,1)}), bf16[8192,2,384]{2,0,1:T(8,128)(2,1)}) %all-gather.5.cloned.1.call-update) | async-done | bytes 12582928 | tf_op jit(solution)/shard_map/all_gather | solution.py:68
  343.5 10.1 %fusion.67 = (bf16[8192,1,384]{2,0,1:T(8,128)(2,1)}, bf16[8192,1,384]{2,0,1:T(8,128)(2,1)}) fusion(bf16[8192,2,384]{2,0,1:T(8,128)(2,1)} %all-gather.5.cloned.1.call-done), kind=kLoop, calls=%fused_computation.85 | loop fusion | bytes 25165824 | tf_op jit(solution)/shard_map/slice | solution.py:76
  353.6 8.7 %copy.73 = bf16[8192,1,384]{0,2,1:T(8,128)(2,1)} copy(bf16[8192,1,384]{2,0,1:T(8,128)(2,1)} %get-tuple-element.15) | data formatting | bytes 12582912 | tf_op jit(solution)/shard_map/slice | solution.py:76
  362.3 4.6 %fusion.75 = (f32[3,128]{1,0:T(4,128)S(1)}, f32[3,128,8192]{2,1,0:T(8,128)S(1)}) fusion(bf16[128,3,128]{0,2,1:T(8,128)(2,1)S(1)} %bitcast.140, bf16[8192,3,128]{0,2,1:T(8,128)(2,1)} %bitcast.130, pred[8192]{0:T(1024)(128)(4,1)S(1)} %get-tuple-element.36), kind=kOutput, calls=%fused_computation.93 | convolution fusion | flops 814743168 | bytes 18982400 | tf_op jit(solution)/shard_map/qhd,khd->hqk/dot_general | solution.py:15
  366.9 11.6 %fusion = (f32[3,128]{1,0:T(4,128)S(1)}, f32[3,128]{1,0:T(4,128)S(1)}) fusion(f32[3,128,8192]{2,1,0:T(8,128)} %get-tuple-element.40, f32[3,128]{1,0:T(4,128)S(1)} %get-tuple-element.34, pred[8192]{0:T(1024)(128)(4,1)S(1)} %get-tuple-element.36, f32[3,128,8192]{2,1,0:T(8,128)S(1)} %get-tuple-element.44, f32[3,128]{1,0:T(4,128)S(1)} %get-tuple-element.32), kind=kLoop, calls=%fused_computation.4 | loop fusion | flops 18873600 | bytes 25180160 | tf_op jit(solution)/shard_map/reduce_sum | solution.py:22
  380.7 8.7 %copy.76 = bf16[8192,1,384]{0,2,1:T(8,128)(2,1)} copy(bf16[8192,1,384]{2,0,1:T(8,128)(2,1)} %get-tuple-element.16) | data formatting | bytes 12582912 | tf_op jit(solution)/shard_map/slice | solution.py:77
  389.3 8.4 %fusion.27 = f32[128,3,128]{0,2,1:T(8,128)S(1)} fusion(bf16[8192,3,128]{0,2,1:T(8,128)(2,1)} %bitcast.132, f32[3,128,8192]{2,1,0:T(8,128)} %copy-done.1, f32[3,128]{1,0:T(4,128)S(1)} %get-tuple-element.32, pred[8192]{0:T(1024)(128)(4,1)S(1)} %get-tuple-element.36), kind=kOutput, calls=%fused_computation.33 | convolution fusion | flops 814743552 | bytes 19080704 | tf_op jit(solution)/shard_map/hqk,khd->qhd/dot_general | solution.py:23
  399.5 7.3 %reduce-scatter.3.cloned.1.call-done = bf16[32,3072]{1,0:T(8,128)(2,1)} async-done(((bf16[128,3072]{1,0:T(8,128)(2,1)}), bf16[32,3072]{1,0:T(8,128)(2,1)}) %reduce-scatter.3.cloned.1.call-update) | async-done | bytes 196624 | tf_op jit(solution)/shard_map/reduce_scatter | solution.py:84
  406.8 24.6 %reduce-scatter.5.cloned.1.call-done = bf16[32,3072]{1,0:T(8,128)(2,1)} async-done(((bf16[128,3072]{1,0:T(8,128)(2,1)}), bf16[32,3072]{1,0:T(8,128)(2,1)}) %reduce-scatter.5.cloned.1.call-update) | async-done | bytes 196624 | tf_op jit(solution)/shard_map/reduce_scatter | solution.py:84
  (48 shorter events, 15.5 us)
Async XLA Ops:
  6.5 372.3 %copy-start = (bf16[384,3072]{1,0:T(8,128)(2,1)S(1)}, bf16[384,3072]{1,0:T(8,128)(2,1)}, u32[]{:S(2)}) copy-start(bf16[384,3072]{1,0:T(8,128)(2,1)} %param.9) | copy-start | bytes 7077892
  6.5 199.0 %all-gather.3.cloned.1.call-start = ((), (), s32[]{:S(2)}) async-start(), calls=%async_computation.4 | async-start | bytes 12779520 | tf_op jit(solution)/shard_map/all_gather | solution.py:68
  8.5 335.0 %all-gather.5.cloned.1.call-start = ((), (), s32[]{:S(2)}) async-start(), calls=%async_computation.6 | async-start | bytes 12779520 | tf_op jit(solution)/shard_map/all_gather | solution.py:68
  17.3 29.7 %copy-start.4 = (s32[256]{0:T(256)S(1)}, s32[256]{0:T(256)}, u32[]{:S(2)}) copy-start(s32[256]{0:T(256)} %param.8) | copy-start | bytes 3076
  43.0 9.5 %all-to-all-start.1 = ((bf16[4,2,18432]{2,1,0:T(2,128)(2,1)}), bf16[4,2,18432]{2,1,0:T(2,128)(2,1)S(1)}, u32[]{:S(2)}, u32[]{:S(2)}) async-start(bf16[4,2,18432]{2,1,0:T(2,128)(2,1)} %reshape.40), calls=%async_computation.2 | async-start | bytes 589824 | tf_op jit(solution)/shard_map/all_to_all | solution.py:47
  47.0 359.8 %reduce-scatter.3.cloned.1.call-start = ((), (), s32[]{:S(2)}) async-start(), calls=%async_computation.5 | async-start | bytes 983040 | tf_op jit(solution)/shard_map/reduce_scatter | solution.py:84
  366.9 11.6 %copy-start.1 = (f32[3,128,8192]{2,1,0:T(8,128)}, f32[3,128,8192]{2,1,0:T(8,128)S(1)}, u32[]{:S(2)}) copy-start(f32[3,128,8192]{2,1,0:T(8,128)S(1)} %get-tuple-element.44) | copy-start | bytes 37748740
  380.4 51.0 %reduce-scatter.5.cloned.1.call-start = ((), (), s32[]{:S(2)}) async-start(), calls=%async_computation.7 | async-start | bytes 983040 | tf_op jit(solution)/shard_map/reduce_scatter | solution.py:84
  389.3 10.2 %copy-start.3 = (f32[2,3072]{1,0:T(2,128)S(1)}, f32[2,3072]{1,0:T(2,128)}, u32[]{:S(2)}) copy-start(f32[2,3072]{1,0:T(2,128)} %param.11) | copy-start | bytes 73732
  389.3 42.0 %copy-start.2 = (bf16[2,32,3072]{2,1,0:T(8,128)(2,1)S(1)}, bf16[2,32,3072]{2,1,0:T(8,128)(2,1)}, u32[]{:S(2)}) copy-start(bf16[2,32,3072]{2,1,0:T(8,128)(2,1)} %param.10) | copy-start | bytes 1179652
  432.5 0.7 copy-start.5
Sparse Core Ops, SparseCore 0:
  10.5 194.9 all-gather.2
  208.7 134.7 all-gather.4
  380.5 26.2 reduce-scatter.2
  409.2 22.1 reduce-scatter.4
where the time goes:
time: 441 us; the launch traced here: 440 us
  waiting for transfers between devices  298 us (68%)
  local copies, waits for them, and re-layouts  67.1 us (15%)
  matrix products  32.4 us (7%)
  between operations  13.3 us (3%)
  other arithmetic  12.9 us (3%)
  blocking collectives  11.4 us (3%)
    all_gather x2, waiting for transfers between devices, shards(): gathered = lax.all_gather(stale_now, 'patch', axis=0, tiled=True)  261 us
    reduce_scatter x2, waiting for transfers between devices, shards(): lax.psum_scatter(jnp.dot(attended, out_weight, preferred_element_type=jnp...  31.8 us
    unnamed x21, local copies, waits for them, and re-layouts  23.6 us
    slice x2, local copies, waits for them, and re-layouts, shards(): gathered[:, 0].reshape(count, local_heads, HEAD_DIM)  18.8 us
    dot_general x4, matrix products, absorb(): jnp.einsum('hqk,khd->qhd', exps.astype(jnp.bfloat16), value_rows, preferr...  17.3 us
    slice x2, local copies, waits for them, and re-layouts, shards(): gathered[:, 1].reshape(count, local_heads, HEAD_DIM)  16.9 us
    dot_general x4, matrix products, absorb(): jnp.einsum('qhd,khd->hqk', queries, key_rows, preferred_element_type=jnp....  12.1 us
    reduce_sum x2, other arithmetic, absorb(): row_total = row_total * factor + jnp.sum(exps, axis=2)  11.7 us
  transfers between devices with their start and end apart: 5, of which 5 were waited for; matrix products, arithmetic and copies ran while one was open for 16% of the time, Pallas kernels for 0%

commit v1 on v0

v1 whole, which is shorter than its diff:
```python
import functools

import jax
import jax.numpy as jnp
from jax import lax
from jax.experimental import pallas as pl
from jax.experimental.pallas import tpu as pltpu
from jax.sharding import PartitionSpec as P

HEAD_DIM = 128
MESH = pl.DeviceIdType.MESH
MASKED = -1e30
SCALE = HEAD_DIM**-0.5 * 1.4426950408889634
BF16 = jnp.bfloat16
F32 = jnp.float32


def device(x, y, z, c):
    return ((z // 2) * 16 + y * 4 + x, (z % 2) * 2 + c)


def plane(z):
    return (z // 2) % 2, 2 * (z % 2) + z // 4


def columns_of(rows):
    count, width = rows.shape
    padded = jnp.concatenate([rows, jnp.zeros((128 - count, width), F32)], axis=0)
    return jnp.transpose(padded)


def as_row(column, width):
    return jnp.transpose(jnp.broadcast_to(column, (width, 128)))[:8]


def attend(queries, keys, values, add_bias):
    scores = lax.dot_general(queries, keys, (((1,), (1,)), ((), ())), preferred_element_type=F32)
    scores = add_bias(scores)
    best = jnp.max(scores, axis=1, keepdims=True) * SCALE
    exps = jnp.exp2(scores * SCALE - best)
    total = jnp.sum(exps, axis=1, keepdims=True)
    summed = jnp.dot(exps.astype(BF16), values, preferred_element_type=F32)
    return (summed / total).astype(BF16), best + jnp.log2(total)


def kernel(
    fresh, stale, mask, weight, inputs, gate, out,
    q, kv, part_out, part_in, stat_out, stat_in, merged, merged_stat, land, land_stat,
    home, own, own_out, own_stat, w_all, att, pair_out, pair_in, kept, bias_own, cols, cols_own,
    zq_s, zq_r, zk_s, zs_s, zk_r, home_s, home_r, w_s, w_r, w_l, xq_s, xq_r, qf_s, qf_r, yk_s, yk_r,
    o_s, o_r, t_s, t_r, b_s, b_r, bt_s, bt_r, own_s, own_r, ot_s, ot_r, p_s, p_r,
):
    patch, head = lax.axis_index("patch"), lax.axis_index("head")
    x, y, zh = patch % 4, (patch // 4) % 4, patch // 16
    zl, c = head // 2, head % 2
    z = zh * 2 + zl
    step_here, group_here = plane(z)
    slot_here = step_here * 2 + group_here % 2
    sibling = device(x, y, z, 1 - c)

    def send(src, dst, ss, rs, to):
        pltpu.make_async_remote_copy(
            src_ref=src, dst_ref=dst, send_sem=ss, recv_sem=rs, device_id=to, device_id_type=MESH
        ).start()

    def wait(ref, sem):
        pltpu.make_async_copy(ref, ref, sem).wait()

    barrier = pltpu.get_barrier_semaphore()

    def greet(to):
        pl.semaphore_signal(barrier, inc=1, device_id=to, device_id_type=MESH)

    greet(sibling)

    @pl.loop(1, 8)
    def _(d):
        greet(device(x, y, (z + d) % 8, 0))
        greet(device(x, y, (z + d) % 8, 1))

    @pl.loop(1, 4)
    def _(d):
        greet(device((x + d) % 4, y, z, 0))
        greet(device((x + d) % 4, y, z, 1))
        greet(device(x, (y + d) % 4, z, c))

    pl.semaphore_wait(barrier, 24)

    stale_plane = 4 * c + zl
    for h in range(3):
        for lane in range(2):
            src = stale.at[:, :, lane, :, pl.ds(h * 128, 128)]
            dst = kv.at[h, :, y, pl.ds(2 * zh, 2)]
            here = jnp.logical_and(stale_plane == z, c == lane)

            @pl.when(here)
            def _():
                pltpu.make_async_copy(src, dst, zk_r.at[h]).start()

            @pl.when(jnp.logical_not(here))
            def _():
                send(src, dst, zs_s.at[h], zk_r.at[h], device(x, y, stale_plane, lane))

        def piece(of_step, kind, group):
            first = pl.multiple_of(group * 384 + h * 128, 128)
            return fresh.at[of_step, kind, :, pl.ds(first, 128)]

        @pl.when(step_here == 1)
        def _():
            pltpu.make_async_copy(piece(0, slice(1, 3), group_here), kv.at[h, :, y, z], zk_r.at[h]).start()

        pltpu.make_async_copy(piece(step_here, 0, group_here), q.at[h, c, 0, z], zq_r.at[h]).start()

        @pl.loop(1, 8)
        def _(d):
            to_z = (z + d) % 8
            to_step, to_group = plane(to_z)
            to = device(x, y, to_z, c)

            @pl.when(to_step == 1)
            def _():
                send(piece(0, slice(1, 3), to_group), kv.at[h, :, y, z], zk_s.at[h], zk_r.at[h], to)

            send(piece(to_step, 0, to_group), q.at[h, c, 0, z], zq_s.at[h], zq_r.at[h], to)

    group = pl.multiple_of(head * 384, 128)
    pltpu.make_async_copy(fresh.at[:, :, :, pl.ds(group, 384)], home.at[:, :, c, zl], home_r.at[0]).start()

    @pl.loop(1, 4)
    def _(d):
        to_head = (head + d) % 4
        first = pl.multiple_of(to_head * 384, 128)
        send(fresh.at[:, :, :, pl.ds(first, 384)], home.at[:, :, c, zl], home_s.at[0], home_r.at[0], (patch, to_head))

    pltpu.make_async_copy(weight, w_all.at[c], w_l.at[0]).start()
    send(weight, w_all.at[c], w_s.at[0], w_r.at[0], sibling)

    mask_row = jnp.where(x == 3, mask[1:2, :], mask[0:1, :])
    text = jnp.where(mask_row == 1, 0.0, MASKED)
    lanes = lax.broadcasted_iota(jnp.int32, (1, 128), 1)
    by_32, by_64, by_96 = (jnp.roll(text, shift, axis=1) for shift in (32, 64, 96))
    low = jnp.where(lanes < 96, by_64, by_32)
    high = jnp.where(lanes < 96, by_32, text)
    text_keys = jnp.where(jnp.logical_and(x >= 2, lanes >= 64), jnp.where(c == 0, low, high), 0.0)
    own_order = jnp.where(lanes < 32, text, jnp.where(lanes < 64, by_96, jnp.where(lanes < 96, by_32, text)))
    own_bias = jnp.where(jnp.logical_and(x >= 2, jnp.logical_and(y == 3, zh == 3)), own_order, 0.0)

    bias_own[...] = jnp.zeros((256, 1024), F32)
    bias_own[:, 896:1024] = jnp.broadcast_to(text_keys, (256, 128))
    same = lax.broadcasted_iota(jnp.int32, (256, 256), 0) // 64 == lax.broadcasted_iota(jnp.int32, (256, 256), 1) // 64
    own_cols = pl.ds(pl.multiple_of(y * 256, 256), 256)
    bias_own[:, own_cols] = jnp.where(same, MASKED, bias_own[:, own_cols])

    for h in range(3):
        wait(kv.at[h, :, y], zk_r.at[h])

        @pl.loop(1, 4)
        def _(d):
            send(kv.at[h, :, y], kv.at[h, :, y], yk_s.at[h], yk_r.at[h, d - 1], device(x, (y + d) % 4, z, c))

        wait(q.at[h, c, 0], zq_r.at[h])

        @pl.loop(1, 4)
        def _(d):
            send(q.at[h, c, 0], q.at[h, c, 4 - d], xq_s.at[h], xq_r.at[h], device((x + d) % 4, y, z, c))

    wait(home, home_r.at[0])
    for s in range(2):
        for h in range(3):
            rows = [home[s, kind, :, :, :, h * 128 : h * 128 + 128].reshape(128, 128) for kind in range(3)]
            block, lse = attend(*rows, lambda scores: scores + own_bias)
            halves = block.reshape(2, 64, 128)
            own[c, s, h] = jnp.where(c == 0, halves[0], halves[1])
            own_out[s, h] = jnp.where(c == 0, halves[1], halves[0])
            own_stat[c, s * 3 + h : s * 3 + h + 1, :] = as_row(lse, 128)[:1]
    send(own_out, own.at[c], own_s.at[0], own_r.at[0], sibling)
    send(own_stat.at[c], own_stat.at[c], ot_s.at[0], ot_r.at[0], sibling)

    for h in range(3):
        wait(q.at[h, c, pl.ds(1, 3)], xq_r.at[h])
        send(q.at[h, c], q.at[h, c], qf_s.at[h], qf_r.at[h], sibling)

    for h in range(3):
        for d in range(1, 4):
            wait(kv.at[h, :, (y + 4 - d) % 4], yk_r.at[h, d - 1])
        wait(q.at[h, 1 - c], qf_r.at[h])

        def tile(r, lane, add_bias):
            keys, values = (kv[h, kind].reshape(1024, 128) for kind in range(2))
            return attend(q[h, lane, r].reshape(256, 128), keys, values, add_bias)

        def text_bias(scores):
            return jnp.concatenate([scores[:, :896], scores[:, 896:] + text_keys], axis=1)

        @pl.loop(2, 8)
        def _(index):
            r, lane = index // 2, index % 2
            block, lse = tile(r, lane, text_bias)
            part_out[h, index - 1] = block
            stat_out[h, index - 1] = as_row(lse, 256)
            to = device((x + r) % 4, y, z, lane)
            slot = (4 - r) * 2 + (c + lane) % 2
            send(part_out.at[h, index - 1], part_in.at[h, slot], o_s.at[h], o_r.at[h], to)
            send(stat_out.at[h, index - 1], stat_in.at[h, slot], t_s.at[h], t_r.at[h], to)

        block, lse = tile(0, 1 - c, lambda scores: scores + bias_own[...])
        part_out[h, 0] = block
        stat_out[h, 0] = as_row(lse, 256)
        send(part_out.at[h, 0], part_in.at[h, 1], o_s.at[h], o_r.at[h], sibling)
        send(stat_out.at[h, 0], stat_in.at[h, 1], t_s.at[h], t_r.at[h], sibling)
        block, lse = tile(0, c, lambda scores: scores + bias_own[...])
        part_in[h, 0] = block
        stat_in[h, 0] = as_row(lse, 256)

    for h in range(3):
        wait(part_in.at[h, pl.ds(1, 7)], o_r.at[h])
        wait(stat_in.at[h, pl.ds(1, 7)], t_r.at[h])
        stats = stat_in[h, :, 0, :]
        best = jnp.max(stats, axis=0, keepdims=True)
        shares = jnp.exp2(stats - best)
        total = jnp.sum(shares, axis=0, keepdims=True)
        share_cols = columns_of(shares / total)
        summed = part_in[h, 0].astype(F32) * share_cols[:, 0:1]
        for i in range(1, 8):
            summed = summed + part_in[h, i].astype(F32) * share_cols[:, i : i + 1]
        merged[h] = summed.astype(BF16).reshape(4, 64, 128)
        merged_stat[h] = jnp.broadcast_to(best + jnp.log2(total), (8, 256))
        pltpu.make_async_copy(merged.at[h, zh], land.at[h, slot_here], b_r.at[h]).start()
        pltpu.make_async_copy(merged_stat.at[h], land_stat.at[h, slot_here], bt_r.at[h]).start()

        @pl.loop(1, 4)
        def _(d):
            to_zh = (zh + d) % 4
            to = device(x, y, 2 * to_zh + zl, c)
            send(merged.at[h, to_zh], land.at[h, slot_here], b_s.at[h], b_r.at[h], to)
            send(merged_stat.at[h], land_stat.at[h, slot_here], bt_s.at[h], bt_r.at[h], to)

    wait(own_out, own_r.at[0])
    wait(own_stat.at[0], ot_r.at[0])
    cols_own[...] = columns_of(own_stat[...].reshape(16, 128))
    own_cols_here = cols_own[pl.ds(pl.multiple_of(c * 64, 64), 64), :]
    for h in range(3):
        wait(land.at[h], b_r.at[h])
        wait(land_stat.at[h], bt_r.at[h])
        cols[...] = columns_of(land_stat[h, :, 0, :])
        cols_here = cols[pl.ds(pl.multiple_of(zh * 64, 64), 64), :]
        for s in range(2):
            for j in range(2):
                lse_far = cols_here[:, s * 2 + j : s * 2 + j + 1]
                at = j * 8 + s * 3 + h
                lse_own = own_cols_here[:, at : at + 1]
                best = jnp.maximum(lse_far, lse_own)
                far, near = jnp.exp2(lse_far - best), jnp.exp2(lse_own - best)
                blended = (land[h, s * 2 + j].astype(F32) * far + own[j, s, h].astype(F32) * near) / (far + near)
                first = j * 384 + h * 128
                att[:, s * 32 : s * 32 + 32, first : first + 128] = blended.astype(BF16).reshape(2, 32, 128)

    wait(weight, w_l.at[0])
    wait(weight, w_r.at[0])
    pair = device(x, y, zh * 2 + 1 - zl, c)

    def project(which, n):
        cut = slice(n * 768, n * 768 + 768)
        return sum(
            jnp.dot(att[which, :, j * 384 : j * 384 + 384], w_all[j, :, cut], preferred_element_type=F32)
            for j in range(2)
        )

    for n in range(4):
        pair_out[n] = project(1 - zl, n).astype(BF16)
        send(pair_out.at[n], pair_in.at[n], p_s.at[n], p_r.at[n], pair)
    for n in range(4):
        kept[n] = project(zl, n)
    for n in range(4):
        wait(pair_in.at[n], p_r.at[n])
        cut = slice(n * 768, n * 768 + 768)
        branch = kept[n] + pair_in[n].astype(F32)
        for s in range(2):
            rows = slice(s * 32, s * 32 + 32)
            out[s, :, cut] = (inputs[s, :, cut].astype(F32) + gate[s : s + 1, cut] * branch[rows]).astype(BF16)

    for h in range(3):
        wait(q.at[h, 0, 0, pl.ds(0, 7)], zq_s.at[h])
        wait(q.at[h, 0, pl.ds(1, 3)], xq_s.at[h])
        wait(q.at[h, 0], qf_s.at[h])
        wait(kv.at[h, :, pl.ds(0, 3)], yk_s.at[h])
        wait(part_out.at[h, pl.ds(0, 7)], o_s.at[h])
        wait(stat_out.at[h, pl.ds(0, 7)], t_s.at[h])
        wait(merged.at[h, pl.ds(0, 3)], b_s.at[h])
        wait(land_stat.at[h, pl.ds(0, 3)], bt_s.at[h])

        @pl.when(step_here == 1)
        def _():
            wait(kv.at[h, :, 0, pl.ds(0, 3)], zk_s.at[h])

        @pl.when(step_here == 0)
        def _():
            wait(kv.at[h, :, 0, pl.ds(0, 4)], zk_s.at[h])

        @pl.when(stale_plane == z)
        def _():
            wait(kv.at[h, :, 0, pl.ds(0, 2)], zs_s.at[h])

        @pl.when(stale_plane != z)
        def _():
            wait(kv.at[h, :, 0, pl.ds(0, 4)], zs_s.at[h])

    wait(home.at[:, :, 0], home_s.at[0])
    wait(home.at[:, :, 0, 0], home_s.at[0])
    wait(weight, w_s.at[0])
    wait(own_out, own_s.at[0])
    wait(own_stat.at[0], ot_s.at[0])
    for n in range(4):
        wait(pair_out.at[n], p_s.at[n])


def shards(fresh_qkv, stale_kv, text_mask, out_weight, inputs, gate):
    fresh = jnp.transpose(fresh_qkv, (0, 2, 1, 3))
    stale = jnp.transpose(stale_kv, (1, 0, 2)).reshape(2, 2, 2, 32, 384)
    vmem, anywhere = pl.BlockSpec(memory_space=pltpu.VMEM), pl.BlockSpec(memory_space=pl.ANY)
    dma = pltpu.SemaphoreType.DMA
    sems = {
        "zq_s": (3,), "zq_r": (3,), "zk_s": (3,), "zs_s": (3,), "zk_r": (3,), "home_s": (1,), "home_r": (1,),
        "w_s": (1,), "w_r": (1,), "w_l": (1,), "xq_s": (3,), "xq_r": (3,), "qf_s": (3,), "qf_r": (3,),
        "yk_s": (3,), "yk_r": (3, 3), "o_s": (3,), "o_r": (3,), "t_s": (3,), "t_r": (3,), "b_s": (3,), "b_r": (3,),
        "bt_s": (3,), "bt_r": (3,), "own_s": (1,), "own_r": (1,), "ot_s": (1,), "ot_r": (1,), "p_s": (4,), "p_r": (4,),
    }
    buffers = {
        "q": ((3, 2, 4, 8, 32, 128), BF16), "kv": ((3, 2, 4, 8, 32, 128), BF16),
        "part_out": ((3, 7, 256, 128), BF16), "part_in": ((3, 8, 256, 128), BF16),
        "stat_out": ((3, 7, 8, 256), F32), "stat_in": ((3, 8, 8, 256), F32),
        "merged": ((3, 4, 64, 128), BF16), "merged_stat": ((3, 8, 256), F32),
        "land": ((3, 4, 64, 128), BF16), "land_stat": ((3, 4, 8, 256), F32),
        "home": ((2, 3, 2, 2, 32, 384), BF16), "own": ((2, 2, 3, 64, 128), BF16), "own_out": ((2, 3, 64, 128), BF16),
        "own_stat": ((2, 8, 128), F32), "w_all": ((2, 384, 3072), BF16), "att": ((2, 64, 768), BF16),
        "pair_out": ((4, 64, 768), BF16), "pair_in": ((4, 64, 768), BF16), "kept": ((4, 64, 768), F32),
        "bias_own": ((256, 1024), F32), "cols": ((256, 128), F32), "cols_own": ((128, 128), F32),
    }
    call = pl.pallas_call(
        kernel,
        out_shape=jax.ShapeDtypeStruct(inputs.shape, BF16),
        in_specs=[anywhere, anywhere, vmem, anywhere, vmem, vmem],
        out_specs=vmem,
        scratch_shapes=[pltpu.VMEM(*spec) for spec in buffers.values()] + [dma(shape) for shape in sems.values()],
        compiler_params=pltpu.CompilerParams(collective_id=0, has_side_effects=True, vmem_limit_bytes=48 << 20),
        name="stale_patch_attention",
    )
    return call(fresh, stale, text_mask.reshape(2, 128), out_weight, inputs, gate)


def solution(mesh):
    placed = (
        P(None, ("patch", "head"), None, None),
        P("patch", None, "head"),
        P(),
        P("head", None),
        P(None, ("patch", "head"), None),
        P(),
    )
    return jax.shard_map(
        shards,
        mesh=mesh,
        in_specs=placed,
        out_specs=P(None, ("patch", "head"), None),
        check_vma=False,
    )
```

time: 441 us -> 78 us (0.18)
  waiting for transfers between devices: 298 us -> 0 us
  Pallas kernels: 0 us -> 70.9 us
  local copies, waits for them, and re-layouts: 67.1 us -> 6.83 us
  matrix products: 32.4 us -> 0 us
  between operations: 13.3 us -> 0.02 us
  other arithmetic: 12.9 us -> 0 us
  blocking collectives: 11.4 us -> 0 us
    all_gather x2 -> x0, waiting for transfers between devices: 261 us -> none  [shards(): gathered = lax.all_gather(stale_now, 'patch', axis=0, tiled=True)]
    pallas_call x0 -> x1, Pallas kernels: none -> 70.9 us  [shards(): call(fresh, stale, text_mask.reshape(2, 128), out_weight, inputs, gate)]
    slice x15 -> x0, local copies, waits for them, and re-layouts: 38.4 us -> none  [the longest x2 18.8 us: shards(): gathered[:, 0].reshape(count, local_heads, HEAD_DIM)]
    dot_general x10 -> x0, matrix products: 32.4 us -> none  [the longest x4 17.3 us: absorb(): jnp.einsum('hqk,khd->qhd', exps.astype(jnp.bfloat16), value_rows, preferr...]
    reduce_scatter x2 -> x0, waiting for transfers between devices: 31.8 us -> none  [shards(): lax.psum_scatter(jnp.dot(attended, out_weight, preferred_element_type=jnp...]
    unnamed x21 -> x11, local copies, waits for them, and re-layouts: 23.6 us -> 5.88 us
    reduce_sum x2 -> x0, other arithmetic: 11.7 us -> none  [absorb(): row_total = row_total * factor + jnp.sum(exps, axis=2)]
    all_to_all x1 -> x0, blocking collectives: 11.4 us -> none  [shards(): lax.all_to_all(fresh_qkv[index], 'head', split_axis=2, concat_axis=0, til...]
  transfers between devices with their start and end apart: 5 -> 0, of which waited for: 5 -> 0; matrix products, arithmetic and copies ran while one was open for 16% -> 0% of each run, Pallas kernels for 0% -> 0%
where the time goes in v1:
time: 78 us; the launch traced here: 77.7 us
  Pallas kernels  70.9 us (91%)
  local copies, waits for them, and re-layouts  6.83 us (9%)
    pallas_call x1, Pallas kernels, shards(): call(fresh, stale, text_mask.reshape(2, 128), out_weight, inputs, gate)  70.9 us
    unnamed x11, local copies, waits for them, and re-layouts  5.88 us

profile of v1, /device:TPU:1, one launch (start us, length us, event | category | flops | bytes accessed | tf_op | source)
XLA Modules:
  0.0 77.7 jit_solution(6847820796623020908)
XLA Ops:
  0.0 0.9 %copy.7 = bf16[2,128,384]{2,1,0:T(8,128)(2,1)S(1)} copy(bf16[2,128,384]{2,0,1:T(2,128)(2,1)} %bitcast.7) | data formatting | bytes 393216 | tf_op jit(solution)/shard_map/transpose | solution.py:319
  1.0 0.0 copy-start
  1.0 1.7 %copy-done = bf16[384,3072]{1,0:T(8,128)(2,1)S(1)} copy-done((bf16[384,3072]{1,0:T(8,128)(2,1)S(1)}, bf16[384,3072]{1,0:T(8,128)(2,1)}, u32[]{:S(2)}) %copy-start) | copy-done | bytes 2359320
  2.6 0.0 copy-start.1
  2.6 1.1 %copy-done.1 = bf16[2,32,3,1536]{3,1,2,0:T(8,128)(2,1)S(1)} copy-done((bf16[2,32,3,1536]{3,1,2,0:T(8,128)(2,1)S(1)}, bf16[2,32,3,1536]{3,1,2,0:T(8,128)(2,1)}, u32[]{:S(2)}) %copy-start.1) | copy-done | bytes 589848
  3.7 0.0 copy-start.2
  3.7 1.0 %copy-done.2 = bf16[2,32,3072]{2,1,0:T(8,128)(2,1)S(1)} copy-done((bf16[2,32,3072]{2,1,0:T(8,128)(2,1)S(1)}, bf16[2,32,3072]{2,1,0:T(8,128)(2,1)}, u32[]{:S(2)}) %copy-start.2) | copy-done | bytes 393240
  4.7 0.0 copy-start.3
  4.7 0.7 copy-done.3
  5.4 0.0 copy-start.4
  5.4 0.7 copy-done.4
  6.1 70.9 %stale_patch_attention.1 = bf16[2,32,3072]{2,1,0:T(8,128)(2,1)S(1)} custom-call(bf16[2,3,32,1536]{3,2,1,0:T(8,128)(2,1)S(1)} %bitcast.5, bf16[2,2,2,32,384]{4,3,2,1,0:T(8,128)(2,1)S(1)} %bitcast.4, s32[2,128]{1,0:T(2,128)S(1)} %bitcast.6, bf16[384,3072]{1,0:T(8,128)(2,1)S(1)} %copy-done, bf16[2,32,3072]{2,1,0:T(8,128)(2,1)S(1)} %copy-done.2, ...), custom_call_target="tpu_custom_call" | custom-call | tf_op jit(solution)/shard_map/stale_patch_attention/pallas_call | solution.py:348
  77.0 0.7 copy.9
Async XLA Ops:
  1.0 1.7 %copy-start = (bf16[384,3072]{1,0:T(8,128)(2,1)S(1)}, bf16[384,3072]{1,0:T(8,128)(2,1)}, u32[]{:S(2)}) copy-start(bf16[384,3072]{1,0:T(8,128)(2,1)} %weight.1) | copy-start | bytes 7077892
  2.6 1.1 %copy-start.1 = (bf16[2,32,3,1536]{3,1,2,0:T(8,128)(2,1)S(1)}, bf16[2,32,3,1536]{3,1,2,0:T(8,128)(2,1)}, u32[]{:S(2)}) copy-start(bf16[2,32,3,1536]{3,1,2,0:T(8,128)(2,1)} %param.6) | copy-start | bytes 1769476
  3.7 1.0 %copy-start.2 = (bf16[2,32,3072]{2,1,0:T(8,128)(2,1)S(1)}, bf16[2,32,3072]{2,1,0:T(8,128)(2,1)}, u32[]{:S(2)}) copy-start(bf16[2,32,3072]{2,1,0:T(8,128)(2,1)} %inputs.1) | copy-start | bytes 1179652
  4.7 0.7 copy-start.3
  5.4 0.7 copy-start.4

commit v2 on v1

--- a/solution.py
+++ b/solution.py
@@ -44,18 +44,19 @@
 
 
 def kernel(
-    fresh, stale, mask, weight, inputs, gate, out,
-    q, kv, part_out, part_in, stat_out, stat_in, merged, merged_stat, land, land_stat,
-    home, own, own_out, own_stat, w_all, att, pair_out, pair_in, kept, bias_own, cols, cols_own,
+    fresh, stale_far, mask, weight, inputs_far, gate_far, out,
+    inputs, gate, stale_raw, stale, q, kv, part_out, part_in, stat_out, stat_in, merged, att,
+    home, own_out, own_in, own_stat_out, own_stat_in, w_all, near_out, near_in, kept, bias_own,
     zq_s, zq_r, zk_s, zs_s, zk_r, home_s, home_r, w_s, w_r, w_l, xq_s, xq_r, qf_s, qf_r, yk_s, yk_r,
-    o_s, o_r, t_s, t_r, b_s, b_r, bt_s, bt_r, own_s, own_r, ot_s, ot_r, p_s, p_r,
+    o_s, o_r, t_s, t_r, b_s, b_r, own_s, own_r, ot_s, ot_r, p_s, p_r, i_l,
 ):
     patch, head = lax.axis_index("patch"), lax.axis_index("head")
     x, y, zh = patch % 4, (patch // 4) % 4, patch // 16
     zl, c = head // 2, head % 2
     z = zh * 2 + zl
     step_here, group_here = plane(z)
-    slot_here = step_here * 2 + group_here % 2
+    to_stale = pltpu.make_async_copy(stale_far, stale_raw, i_l.at[2])
+    to_stale.start()
     sibling = device(x, y, z, 1 - c)
 
     def send(src, dst, ss, rs, to):
@@ -84,10 +85,13 @@
         greet(device((x + d) % 4, y, z, 1))
         greet(device(x, (y + d) % 4, z, c))
 
+    to_stale.wait()
+    for kind in range(2):
+        stale[kind] = stale_raw[:, kind, :].reshape(2, 2, 32, 384)
     pl.semaphore_wait(barrier, 24)
 
     stale_plane = 4 * c + zl
-    for h in range(3):
+    def spread(h):
         for lane in range(2):
             src = stale.at[:, :, lane, :, pl.ds(h * 128, 128)]
             dst = kv.at[h, :, y, pl.ds(2 * zh, 2)]
@@ -123,16 +127,12 @@
 
             send(piece(to_step, 0, to_group), q.at[h, c, 0, z], zq_s.at[h], zq_r.at[h], to)
 
-    group = pl.multiple_of(head * 384, 128)
-    pltpu.make_async_copy(fresh.at[:, :, :, pl.ds(group, 384)], home.at[:, :, c, zl], home_r.at[0]).start()
-
-    @pl.loop(1, 4)
-    def _(d):
-        to_head = (head + d) % 4
-        first = pl.multiple_of(to_head * 384, 128)
-        send(fresh.at[:, :, :, pl.ds(first, 384)], home.at[:, :, c, zl], home_s.at[0], home_r.at[0], (patch, to_head))
+    spread(0)
+    spread(1)
 
     pltpu.make_async_copy(weight, w_all.at[c], w_l.at[0]).start()
+    pltpu.make_async_copy(inputs_far, inputs, i_l.at[0]).start()
+    pltpu.make_async_copy(gate_far, gate, i_l.at[1]).start()
     send(weight, w_all.at[c], w_s.at[0], w_r.at[0], sibling)
 
     mask_row = jnp.where(x == 3, mask[1:2, :], mask[0:1, :])
@@ -151,7 +151,7 @@
     own_cols = pl.ds(pl.multiple_of(y * 256, 256), 256)
     bias_own[:, own_cols] = jnp.where(same, MASKED, bias_own[:, own_cols])
 
-    for h in range(3):
+    def gather(h):
         wait(kv.at[h, :, y], zk_r.at[h])
 
         @pl.loop(1, 4)
@@ -164,23 +164,52 @@
         def _(d):
             send(q.at[h, c, 0], q.at[h, c, 4 - d], xq_s.at[h], xq_r.at[h], device((x + d) % 4, y, z, c))
 
-    wait(home, home_r.at[0])
-    for s in range(2):
-        for h in range(3):
-            rows = [home[s, kind, :, :, :, h * 128 : h * 128 + 128].reshape(128, 128) for kind in range(3)]
-            block, lse = attend(*rows, lambda scores: scores + own_bias)
-            halves = block.reshape(2, 64, 128)
-            own[c, s, h] = jnp.where(c == 0, halves[0], halves[1])
-            own_out[s, h] = jnp.where(c == 0, halves[1], halves[0])
-            own_stat[c, s * 3 + h : s * 3 + h + 1, :] = as_row(lse, 128)[:1]
-    send(own_out, own.at[c], own_s.at[0], own_r.at[0], sibling)
-    send(own_stat.at[c], own_stat.at[c], ot_s.at[0], ot_r.at[0], sibling)
-
-    for h in range(3):
+    gather(0)
+    spread(2)
+    gather(1)
+
+    group = pl.multiple_of(head * 384, 128)
+    pltpu.make_async_copy(fresh.at[:, :, :, pl.ds(group, 384)], home.at[:, :, c, zl], home_r.at[0]).start()
+
+    @pl.loop(1, 4)
+    def _(d):
+        to_head = (head + d) % 4
+        first = pl.multiple_of(to_head * 384, 128)
+        send(fresh.at[:, :, :, pl.ds(first, 384)], home.at[:, :, c, zl], home_s.at[0], home_r.at[0], (patch, to_head))
+
+    def pass_queries(h):
         wait(q.at[h, c, pl.ds(1, 3)], xq_r.at[h])
         send(q.at[h, c], q.at[h, c], qf_s.at[h], qf_r.at[h], sibling)
 
-    for h in range(3):
+    pass_queries(0)
+    gather(2)
+
+    def attend_home():
+        wait(home, home_r.at[0])
+        for s in range(2):
+            for h in range(3):
+                rows = [home[s, kind, :, :, :, h * 128 : h * 128 + 128].reshape(128, 128) for kind in range(3)]
+                block, lse = attend(*rows, lambda scores: scores + own_bias)
+                lses = as_row(lse, 128)[:1]
+                for lane in range(2):
+                    own_out[s, lane, h] = block[lane * 64 : lane * 64 + 64]
+                    own_stat_out[s, lane, h : h + 1, :] = lses if lane == 0 else jnp.roll(lses, 64, axis=1)
+            for lane in range(2):
+                to_z = 4 * c + 2 * s + zl
+                here = jnp.logical_and(to_z == z, c == lane)
+                to = device(x, y, to_z, lane)
+
+                @pl.when(here)
+                def _():
+                    pltpu.make_async_copy(own_out.at[s, lane], own_in.at[:, zh], own_r.at[0]).start()
+                    pltpu.make_async_copy(own_stat_out.at[s, lane], own_stat_in.at[zh], ot_r.at[0]).start()
+
+                @pl.when(jnp.logical_not(here))
+                def _():
+                    send(own_out.at[s, lane], own_in.at[:, zh], own_s.at[0], own_r.at[0], to)
+                    send(own_stat_out.at[s, lane], own_stat_in.at[zh], ot_s.at[0], ot_r.at[0], to)
+
+    def attend_far(h):
         for d in range(1, 4):
             wait(kv.at[h, :, (y + 4 - d) % 4], yk_r.at[h, d - 1])
         wait(q.at[h, 1 - c], qf_r.at[h])
@@ -212,72 +241,73 @@
         part_in[h, 0] = block
         stat_in[h, 0] = as_row(lse, 256)
 
-    for h in range(3):
+    def merge(h):
         wait(part_in.at[h, pl.ds(1, 7)], o_r.at[h])
         wait(stat_in.at[h, pl.ds(1, 7)], t_r.at[h])
-        stats = stat_in[h, :, 0, :]
-        best = jnp.max(stats, axis=0, keepdims=True)
-        shares = jnp.exp2(stats - best)
-        total = jnp.sum(shares, axis=0, keepdims=True)
-        share_cols = columns_of(shares / total)
-        summed = part_in[h, 0].astype(F32) * share_cols[:, 0:1]
-        for i in range(1, 8):
+        pairs = [jnp.where(lanes < 64, own_stat_in[2 * i, h : h + 1, :], jnp.roll(own_stat_in[2 * i + 1, h : h + 1, :], 64, axis=1)) for i in range(2)]
+        stats = jnp.concatenate([stat_in[h, :, 0, :], jnp.concatenate(pairs, axis=1)], axis=0)
+        shares = jnp.exp2(stats - jnp.max(stats, axis=0, keepdims=True))
+        share_cols = columns_of(shares / jnp.sum(shares, axis=0, keepdims=True))
+        summed = own_in[h].reshape(256, 128).astype(F32) * share_cols[:, 8:9]
+        for i in range(8):
             summed = summed + part_in[h, i].astype(F32) * share_cols[:, i : i + 1]
-        merged[h] = summed.astype(BF16).reshape(4, 64, 128)
-        merged_stat[h] = jnp.broadcast_to(best + jnp.log2(total), (8, 256))
-        pltpu.make_async_copy(merged.at[h, zh], land.at[h, slot_here], b_r.at[h]).start()
-        pltpu.make_async_copy(merged_stat.at[h], land_stat.at[h, slot_here], bt_r.at[h]).start()
+        block = summed.astype(BF16)
+        merged[h, 16:272] = block
+        merged[h, 0:16] = block[240:256]
+        merged[h, 272:288] = block[0:16]
+        dst = att.at[step_here, group_here % 2, h]
+
+        def window(to_z):
+            return merged.at[h, pl.ds(pl.multiple_of(to_z * 32, 32), 64)]
+
+        pltpu.make_async_copy(window(z), dst, b_r.at[h]).start()
 
         @pl.loop(1, 4)
         def _(d):
-            to_zh = (zh + d) % 4
-            to = device(x, y, 2 * to_zh + zl, c)
-            send(merged.at[h, to_zh], land.at[h, slot_here], b_s.at[h], b_r.at[h], to)
-            send(merged_stat.at[h], land_stat.at[h, slot_here], bt_s.at[h], bt_r.at[h], to)
-
-    wait(own_out, own_r.at[0])
-    wait(own_stat.at[0], ot_r.at[0])
-    cols_own[...] = columns_of(own_stat[...].reshape(16, 128))
-    own_cols_here = cols_own[pl.ds(pl.multiple_of(c * 64, 64), 64), :]
-    for h in range(3):
-        wait(land.at[h], b_r.at[h])
-        wait(land_stat.at[h], bt_r.at[h])
-        cols[...] = columns_of(land_stat[h, :, 0, :])
-        cols_here = cols[pl.ds(pl.multiple_of(zh * 64, 64), 64), :]
-        for s in range(2):
-            for j in range(2):
-                lse_far = cols_here[:, s * 2 + j : s * 2 + j + 1]
-                at = j * 8 + s * 3 + h
-                lse_own = own_cols_here[:, at : at + 1]
-                best = jnp.maximum(lse_far, lse_own)
-                far, near = jnp.exp2(lse_far - best), jnp.exp2(lse_own - best)
-                blended = (land[h, s * 2 + j].astype(F32) * far + own[j, s, h].astype(F32) * near) / (far + near)
-                first = j * 384 + h * 128
-                att[:, s * 32 : s * 32 + 32, first : first + 128] = blended.astype(BF16).reshape(2, 32, 128)
-
+            to_z = (z + 2 * d) % 8
+            send(window(to_z), dst, b_s.at[h], b_r.at[h], device(x, y, to_z, c))
+
+    attend_far(0)
+    pass_queries(1)
+    attend_home()
+    attend_far(1)
+    pass_queries(2)
+    wait(own_in, own_r.at[0])
+    wait(own_stat_in, ot_r.at[0])
+    merge(0)
+    attend_far(2)
+    merge(1)
+    merge(2)
+
+    wait(inputs, i_l.at[0])
+    wait(gate, i_l.at[1])
     wait(weight, w_l.at[0])
     wait(weight, w_r.at[0])
-    pair = device(x, y, zh * 2 + 1 - zl, c)
-
-    def project(which, n):
+    for h in range(3):
+        wait(att.at[:, :, h], b_r.at[h])
+    blocks = [jnp.concatenate([att[s, j, h] for j in range(2) for h in range(3)], axis=1) for s in range(2)]
+    near = jnp.concatenate([block[rows] for rows in (slice(0, 16), slice(48, 64)) for block in blocks], axis=0)
+    mine = jnp.concatenate([block[16:48] for block in blocks], axis=0)
+
+    def project(rows, n):
         cut = slice(n * 768, n * 768 + 768)
         return sum(
-            jnp.dot(att[which, :, j * 384 : j * 384 + 384], w_all[j, :, cut], preferred_element_type=F32)
-            for j in range(2)
+            jnp.dot(rows[:, j * 384 : j * 384 + 384], w_all[j, :, cut], preferred_element_type=F32) for j in range(2)
         )
 
     for n in range(4):
-        pair_out[n] = project(1 - zl, n).astype(BF16)
-        send(pair_out.at[n], pair_in.at[n], p_s.at[n], p_r.at[n], pair)
+        near_out[n] = project(near, n).astype(BF16).reshape(2, 2, 16, 768)
+        send(near_out.at[n, 0], near_in.at[n, 1], p_s.at[n], p_r.at[n], device(x, y, (z + 7) % 8, c))
+        send(near_out.at[n, 1], near_in.at[n, 0], p_s.at[n], p_r.at[n], device(x, y, (z + 1) % 8, c))
     for n in range(4):
-        kept[n] = project(zl, n)
+        kept[n] = project(mine, n)
     for n in range(4):
-        wait(pair_in.at[n], p_r.at[n])
+        wait(near_in.at[n], p_r.at[n])
         cut = slice(n * 768, n * 768 + 768)
-        branch = kept[n] + pair_in[n].astype(F32)
         for s in range(2):
-            rows = slice(s * 32, s * 32 + 32)
-            out[s, :, cut] = (inputs[s, :, cut].astype(F32) + gate[s : s + 1, cut] * branch[rows]).astype(BF16)
+            other = jnp.concatenate([near_in[n, 0, s], near_in[n, 1, s]], axis=0).astype(F32)
+            branch = kept[n, s * 32 : s * 32 + 32] + other
+            out[s, :, cut] = (inputs[s, :, cut].astype(F32) + gate[s : s + 1, cut] * branch).astype(BF16)
 
     for h in range(3):
         wait(q.at[h, 0, 0, pl.ds(0, 7)], zq_s.at[h])
@@ -286,8 +316,7 @@
         wait(kv.at[h, :, pl.ds(0, 3)], yk_s.at[h])
         wait(part_out.at[h, pl.ds(0, 7)], o_s.at[h])
         wait(stat_out.at[h, pl.ds(0, 7)], t_s.at[h])
-        wait(merged.at[h, pl.ds(0, 3)], b_s.at[h])
-        wait(land_stat.at[h, pl.ds(0, 3)], bt_s.at[h])
+        wait(merged.at[h, pl.ds(0, 192)], b_s.at[h])
 
         @pl.when(step_here == 1)
         def _():
@@ -308,44 +337,54 @@
     wait(home.at[:, :, 0], home_s.at[0])
     wait(home.at[:, :, 0, 0], home_s.at[0])
     wait(weight, w_s.at[0])
-    wait(own_out, own_s.at[0])
-    wait(own_stat.at[0], ot_s.at[0])
+
+    @pl.when(zh // 2 == c)
+    def _():
+        wait(own_in.at[:, pl.ds(0, 3)], own_s.at[0])
+        wait(own_stat_in.at[pl.ds(0, 3)], ot_s.at[0])
+
+    @pl.when(zh // 2 != c)
+    def _():
+        wait(own_in, own_s.at[0])
+        wait(own_stat_in, ot_s.at[0])
+
     for n in range(4):
-        wait(pair_out.at[n], p_s.at[n])
+        wait(near_out.at[n], p_s.at[n])
 
 
 def shards(fresh_qkv, stale_kv, text_mask, out_weight, inputs, gate):
     fresh = jnp.transpose(fresh_qkv, (0, 2, 1, 3))
-    stale = jnp.transpose(stale_kv, (1, 0, 2)).reshape(2, 2, 2, 32, 384)
     vmem, anywhere = pl.BlockSpec(memory_space=pltpu.VMEM), pl.BlockSpec(memory_space=pl.ANY)
     dma = pltpu.SemaphoreType.DMA
     sems = {
         "zq_s": (3,), "zq_r": (3,), "zk_s": (3,), "zs_s": (3,), "zk_r": (3,), "home_s": (1,), "home_r": (1,),
         "w_s": (1,), "w_r": (1,), "w_l": (1,), "xq_s": (3,), "xq_r": (3,), "qf_s": (3,), "qf_r": (3,),
         "yk_s": (3,), "yk_r": (3, 3), "o_s": (3,), "o_r": (3,), "t_s": (3,), "t_r": (3,), "b_s": (3,), "b_r": (3,),
-        "bt_s": (3,), "bt_r": (3,), "own_s": (1,), "own_r": (1,), "ot_s": (1,), "ot_r": (1,), "p_s": (4,), "p_r": (4,),
+        "own_s": (1,), "own_r": (1,), "ot_s": (1,), "ot_r": (1,), "p_s": (4,), "p_r": (4,),
+        "i_l": (3,),
     }
     buffers = {
+        "inputs": ((2, 32, 3072), BF16), "gate": ((2, 3072), F32), "stale_raw": ((128, 2, 384), BF16),
+        "stale": ((2, 2, 2, 32, 384), BF16),
         "q": ((3, 2, 4, 8, 32, 128), BF16), "kv": ((3, 2, 4, 8, 32, 128), BF16),
         "part_out": ((3, 7, 256, 128), BF16), "part_in": ((3, 8, 256, 128), BF16),
         "stat_out": ((3, 7, 8, 256), F32), "stat_in": ((3, 8, 8, 256), F32),
-        "merged": ((3, 4, 64, 128), BF16), "merged_stat": ((3, 8, 256), F32),
-        "land": ((3, 4, 64, 128), BF16), "land_stat": ((3, 4, 8, 256), F32),
-        "home": ((2, 3, 2, 2, 32, 384), BF16), "own": ((2, 2, 3, 64, 128), BF16), "own_out": ((2, 3, 64, 128), BF16),
-        "own_stat": ((2, 8, 128), F32), "w_all": ((2, 384, 3072), BF16), "att": ((2, 64, 768), BF16),
-        "pair_out": ((4, 64, 768), BF16), "pair_in": ((4, 64, 768), BF16), "kept": ((4, 64, 768), F32),
-        "bias_own": ((256, 1024), F32), "cols": ((256, 128), F32), "cols_own": ((128, 128), F32),
+        "merged": ((3, 288, 128), BF16), "att": ((2, 2, 3, 64, 128), BF16),
+        "home": ((2, 3, 2, 2, 32, 384), BF16), "own_out": ((2, 2, 3, 64, 128), BF16), "own_in": ((3, 4, 64, 128), BF16),
+        "own_stat_out": ((2, 2, 8, 128), F32), "own_stat_in": ((4, 8, 128), F32), "w_all": ((2, 384, 3072), BF16),
+        "near_out": ((4, 2, 2, 16, 768), BF16), "near_in": ((4, 2, 2, 16, 768), BF16), "kept": ((4, 64, 768), F32),
+        "bias_own": ((256, 1024), F32),
     }
     call = pl.pallas_call(
         kernel,
         out_shape=jax.ShapeDtypeStruct(inputs.shape, BF16),
-        in_specs=[anywhere, anywhere, vmem, anywhere, vmem, vmem],
+        in_specs=[anywhere, anywhere, vmem, anywhere, anywhere, anywhere],
         out_specs=vmem,
         scratch_shapes=[pltpu.VMEM(*spec) for spec in buffers.values()] + [dma(shape) for shape in sems.values()],
-        compiler_params=pltpu.CompilerParams(collective_id=0, has_side_effects=True, vmem_limit_bytes=48 << 20),
+        compiler_params=pltpu.CompilerParams(collective_id=0, has_side_effects=True, vmem_limit_bytes=60 << 20),
         name="stale_patch_attention",
     )
-    return call(fresh, stale, text_mask.reshape(2, 128), out_weight, inputs, gate)
+    return call(fresh, stale_kv, text_mask.reshape(2, 128), out_weight, inputs, gate)
 
 
 def solution(mesh):

time: 78 us -> 66.4 us (0.85)
  Pallas kernels: 70.9 us -> 64.5 us
  local copies, waits for them, and re-layouts: 6.83 us -> 1.77 us
    pallas_call x1, Pallas kernels: 70.9 us -> 64.5 us  [shards(): call(fresh, stale_kv, text_mask.reshape(2, 128), out_weight, inputs, gate)]
    unnamed x11 -> x1, local copies, waits for them, and re-layouts: 5.88 us -> 1.77 us
    transpose x1 -> x0, local copies, waits for them, and re-layouts: 0.95 us -> none  [shards(): stale = jnp.transpose(stale_kv, (1, 0, 2)).reshape(2, 2, 2, 32, 384)]
where the time goes in v2:
time: 66.4 us; the launch traced here: 66.2 us
  Pallas kernels  64.5 us (97%)
  local copies, waits for them, and re-layouts  1.77 us (3%)
    pallas_call x1, Pallas kernels, shards(): call(fresh, stale_kv, text_mask.reshape(2, 128), out_weight, inputs, gate)  64.5 us
    unnamed x1, local copies, waits for them, and re-layouts  1.77 us

profile of v2, /device:TPU:1, one launch (start us, length us, event | category | flops | bytes accessed | tf_op | source)
XLA Modules:
  0.0 66.2 jit_solution(1966442191431725327)
XLA Ops:
  0.0 64.5 %stale_patch_attention.1 = bf16[2,32,3072]{2,1,0:T(8,128)(2,1)} custom-call(bf16[2,3,32,1536]{3,2,1,0:T(8,128)(2,1)} %bitcast.2, bf16[128,2,384]{2,1,0:T(2,128)(2,1)} %stale_far.1, s32[2,128]{1,0:T(2,128)} %bitcast.3, bf16[384,3072]{1,0:T(8,128)(2,1)} %weight.1, bf16[2,32,3072]{2,1,0:T(8,128)(2,1)} %inputs_far.1, f32[2,3072]{1,0:T(2,128)} %gate_far.1), custom_call_target="tpu_custom_call" | custom-call | tf_op jit(solution)/shard_map/stale_patch_attention/pallas_call | solution.py:387
  64.5 1.8 %copy.8 = bf16[2,32,3072]{2,1,0:T(8,128)(2,1)} copy(bf16[2,32,3072]{2,1,0:T(8,128)(2,1)} %stale_patch_attention.1) | data formatting | bytes 786432

commit v3 on v2

--- a/solution.py
+++ b/solution.py
@@ -33,21 +33,23 @@
     return jnp.transpose(jnp.broadcast_to(column, (width, 128)))[:8]
 
 
-def attend(queries, keys, values, add_bias):
-    scores = lax.dot_general(queries, keys, (((1,), (1,)), ((), ())), preferred_element_type=F32)
-    scores = add_bias(scores)
+def score(queries, keys):
+    return lax.dot_general(queries, keys, (((1,), (1,)), ((), ())), preferred_element_type=F32)
+
+
+def weigh(scores, values):
     best = jnp.max(scores, axis=1, keepdims=True) * SCALE
     exps = jnp.exp2(scores * SCALE - best)
     total = jnp.sum(exps, axis=1, keepdims=True)
     summed = jnp.dot(exps.astype(BF16), values, preferred_element_type=F32)
-    return (summed / total).astype(BF16), best + jnp.log2(total)
+    return summed / total, best + jnp.log2(total)
 
 
 def kernel(
-    fresh, stale_far, mask, weight, inputs_far, gate_far, out,
-    inputs, gate, stale_raw, stale, q, kv, part_out, part_in, stat_out, stat_in, merged, att,
-    home, own_out, own_in, own_stat_out, own_stat_in, w_all, near_out, near_in, kept, bias_own,
-    zq_s, zq_r, zk_s, zs_s, zk_r, home_s, home_r, w_s, w_r, w_l, xq_s, xq_r, qf_s, qf_r, yk_s, yk_r,
+    fresh_far, stale_far, mask, weight, inputs_far, gate_far, out,
+    inputs, gate, fresh, stale_raw, stale, q, kv, side_out, side_in, side_stat_out, side_stat_in, part_out, part_in, stat_out, stat_in, merged, att,
+    home, own_out, own_in, own_stat_out, own_stat_in, w_all, near_out, near_in, kept, bias_own, held,
+    zq_s, zq_r, zk_s, zs_s, zk_r, home_s, home_r, w_s, w_r, w_l, xq_s, xq_r, qf_s, qf_r, yk_s, yk_r, so_s, so_r, st_s, st_r,
     o_s, o_r, t_s, t_r, b_s, b_r, own_s, own_r, ot_s, ot_r, p_s, p_r, i_l,
 ):
     patch, head = lax.axis_index("patch"), lax.axis_index("head")
@@ -57,6 +59,8 @@
     step_here, group_here = plane(z)
     to_stale = pltpu.make_async_copy(stale_far, stale_raw, i_l.at[2])
     to_stale.start()
+    to_fresh = pltpu.make_async_copy(fresh_far, fresh, i_l.at[3])
+    to_fresh.start()
     sibling = device(x, y, z, 1 - c)
 
     def send(src, dst, ss, rs, to):
@@ -81,20 +85,29 @@
 
     @pl.loop(1, 4)
     def _(d):
-        greet(device((x + d) % 4, y, z, 0))
-        greet(device((x + d) % 4, y, z, 1))
+        greet(device((x + d) % 4, y, z, c))
         greet(device(x, (y + d) % 4, z, c))
 
     to_stale.wait()
+    to_fresh.wait()
     for kind in range(2):
         stale[kind] = stale_raw[:, kind, :].reshape(2, 2, 32, 384)
-    pl.semaphore_wait(barrier, 24)
+    pl.semaphore_wait(barrier, 21)
+
+    def query_peer(h, d):
+        return device(x, (y + d) % 4, z, c) if h == 1 else device((x + d) % 4, y, z, c)
+
+    def key_peer(h, d):
+        return query_peer(1 - h % 2, d)
+
+    def key_slot(h):
+        return x if h == 1 else y
 
     stale_plane = 4 * c + zl
     def spread(h):
         for lane in range(2):
             src = stale.at[:, :, lane, :, pl.ds(h * 128, 128)]
-            dst = kv.at[h, :, y, pl.ds(2 * zh, 2)]
+            dst = kv.at[h, :, key_slot(h), pl.ds(2 * zh, 2)]
             here = jnp.logical_and(stale_plane == z, c == lane)
 
             @pl.when(here)
@@ -111,7 +124,7 @@
 
         @pl.when(step_here == 1)
         def _():
-            pltpu.make_async_copy(piece(0, slice(1, 3), group_here), kv.at[h, :, y, z], zk_r.at[h]).start()
+            pltpu.make_async_copy(piece(0, slice(1, 3), group_here), kv.at[h, :, key_slot(h), z], zk_r.at[h]).start()
 
         pltpu.make_async_copy(piece(step_here, 0, group_here), q.at[h, c, 0, z], zq_r.at[h]).start()
 
@@ -123,49 +136,63 @@
 
             @pl.when(to_step == 1)
             def _():
-                send(piece(0, slice(1, 3), to_group), kv.at[h, :, y, z], zk_s.at[h], zk_r.at[h], to)
-
-            send(piece(to_step, 0, to_group), q.at[h, c, 0, z], zq_s.at[h], zq_r.at[h], to)
+                send(piece(0, slice(1, 3), to_group), kv.at[h, :, key_slot(h), z], zk_s.at[h], zk_r.at[h], to)
+
+        @pl.loop(1, 8)
+        def _(d):
+            to_z = (z + d) % 8
+            to_step, to_group = plane(to_z)
+            send(piece(to_step, 0, to_group), q.at[h, c, 0, z], zq_s.at[h], zq_r.at[h], device(x, y, to_z, c))
 
     spread(0)
     spread(1)
+    spread(2)
 
     pltpu.make_async_copy(weight, w_all.at[c], w_l.at[0]).start()
     pltpu.make_async_copy(inputs_far, inputs, i_l.at[0]).start()
     pltpu.make_async_copy(gate_far, gate, i_l.at[1]).start()
     send(weight, w_all.at[c], w_s.at[0], w_r.at[0], sibling)
 
-    mask_row = jnp.where(x == 3, mask[1:2, :], mask[0:1, :])
-    text = jnp.where(mask_row == 1, 0.0, MASKED)
-    lanes = lax.broadcasted_iota(jnp.int32, (1, 128), 1)
+    text = jnp.where(mask[...] == 1, 0.0, MASKED)
+    lanes = lax.broadcasted_iota(jnp.int32, (2, 128), 1)
     by_32, by_64, by_96 = (jnp.roll(text, shift, axis=1) for shift in (32, 64, 96))
     low = jnp.where(lanes < 96, by_64, by_32)
     high = jnp.where(lanes < 96, by_32, text)
-    text_keys = jnp.where(jnp.logical_and(x >= 2, lanes >= 64), jnp.where(c == 0, low, high), 0.0)
+    text_keys = jnp.where(lanes >= 64, jnp.where(c == 0, low, high), 0.0)
+    of_column = jnp.where(x >= 2, jnp.where(x == 3, text_keys[1:2], text_keys[0:1]), 0.0)
+    of_row = jnp.where(y == 3, text_keys, 0.0)
+    far_biases = [[(7, of_column)], [(5, of_row[0:1]), (7, of_row[1:2])]]
     own_order = jnp.where(lanes < 32, text, jnp.where(lanes < 64, by_96, jnp.where(lanes < 96, by_32, text)))
+    own_order = jnp.where(x == 3, own_order[1:2], own_order[0:1])
     own_bias = jnp.where(jnp.logical_and(x >= 2, jnp.logical_and(y == 3, zh == 3)), own_order, 0.0)
 
-    bias_own[...] = jnp.zeros((256, 1024), F32)
-    bias_own[:, 896:1024] = jnp.broadcast_to(text_keys, (256, 128))
+    def far_bias(h, scores):
+        blocks = [scores[:, i * 128 : i * 128 + 128] for i in range(8)]
+        for i, bias in far_biases[h % 2]:
+            blocks[i] = blocks[i] + bias
+        return jnp.concatenate(blocks, axis=1)
+
     same = lax.broadcasted_iota(jnp.int32, (256, 256), 0) // 64 == lax.broadcasted_iota(jnp.int32, (256, 256), 1) // 64
-    own_cols = pl.ds(pl.multiple_of(y * 256, 256), 256)
-    bias_own[:, own_cols] = jnp.where(same, MASKED, bias_own[:, own_cols])
+    for h in range(2):
+        bias_own[h] = far_bias(h, jnp.zeros((256, 1024), F32))
+        own_cols = pl.ds(pl.multiple_of(key_slot(h) * 256, 256), 256)
+        bias_own[h, :, own_cols] = jnp.where(same, MASKED, bias_own[h, :, own_cols])
 
     def gather(h):
-        wait(kv.at[h, :, y], zk_r.at[h])
+        slot = key_slot(h)
+        wait(kv.at[h, :, slot], zk_r.at[h])
 
         @pl.loop(1, 4)
         def _(d):
-            send(kv.at[h, :, y], kv.at[h, :, y], yk_s.at[h], yk_r.at[h, d - 1], device(x, (y + d) % 4, z, c))
+            send(kv.at[h, :, slot], kv.at[h, :, slot], yk_s.at[h], yk_r.at[h, d - 1], key_peer(h, d))
 
         wait(q.at[h, c, 0], zq_r.at[h])
 
         @pl.loop(1, 4)
         def _(d):
-            send(q.at[h, c, 0], q.at[h, c, 4 - d], xq_s.at[h], xq_r.at[h], device((x + d) % 4, y, z, c))
+            send(q.at[h, c, 0], q.at[h, c, 4 - d], xq_s.at[h], xq_r.at[h], query_peer(h, d))
 
     gather(0)
-    spread(2)
     gather(1)
 
     group = pl.multiple_of(head * 384, 128)
@@ -189,10 +216,10 @@
         for s in range(2):
             for h in range(3):
                 rows = [home[s, kind, :, :, :, h * 128 : h * 128 + 128].reshape(128, 128) for kind in range(3)]
-                block, lse = attend(*rows, lambda scores: scores + own_bias)
+                block, lse = weigh(score(rows[0], rows[1]) + own_bias, rows[2])
                 lses = as_row(lse, 128)[:1]
                 for lane in range(2):
-                    own_out[s, lane, h] = block[lane * 64 : lane * 64 + 64]
+                    own_out[s, lane, h] = block[lane * 64 : lane * 64 + 64].astype(BF16)
                     own_stat_out[s, lane, h : h + 1, :] = lses if lane == 0 else jnp.roll(lses, 64, axis=1)
             for lane in range(2):
                 to_z = 4 * c + 2 * s + zl
@@ -211,45 +238,54 @@
 
     def attend_far(h):
         for d in range(1, 4):
-            wait(kv.at[h, :, (y + 4 - d) % 4], yk_r.at[h, d - 1])
+            wait(kv.at[h, :, (key_slot(h) + 4 - d) % 4], yk_r.at[h, d - 1])
         wait(q.at[h, 1 - c], qf_r.at[h])
 
-        def tile(r, lane, add_bias):
-            keys, values = (kv[h, kind].reshape(1024, 128) for kind in range(2))
-            return attend(q[h, lane, r].reshape(256, 128), keys, values, add_bias)
-
-        def text_bias(scores):
-            return jnp.concatenate([scores[:, :896], scores[:, 896:] + text_keys], axis=1)
-
-        @pl.loop(2, 8)
-        def _(index):
-            r, lane = index // 2, index % 2
-            block, lse = tile(r, lane, text_bias)
-            part_out[h, index - 1] = block
-            stat_out[h, index - 1] = as_row(lse, 256)
-            to = device((x + r) % 4, y, z, lane)
-            slot = (4 - r) * 2 + (c + lane) % 2
-            send(part_out.at[h, index - 1], part_in.at[h, slot], o_s.at[h], o_r.at[h], to)
-            send(stat_out.at[h, index - 1], stat_in.at[h, slot], t_s.at[h], t_r.at[h], to)
-
-        block, lse = tile(0, 1 - c, lambda scores: scores + bias_own[...])
-        part_out[h, 0] = block
-        stat_out[h, 0] = as_row(lse, 256)
-        send(part_out.at[h, 0], part_in.at[h, 1], o_s.at[h], o_r.at[h], sibling)
-        send(stat_out.at[h, 0], stat_in.at[h, 1], t_s.at[h], t_r.at[h], sibling)
-        block, lse = tile(0, c, lambda scores: scores + bias_own[...])
-        part_in[h, 0] = block
-        stat_in[h, 0] = as_row(lse, 256)
+        tiles = [(r, lane) for lane in (1 - c, c) for r in (1, 2, 3, 0)]
+
+        def score_tile(i):
+            r, lane = tiles[i]
+            scores = score(q[h, lane, r].reshape(256, 128), kv[h, 0].reshape(1024, 128))
+            held[i % 2] = far_bias(h, scores) if r else scores + bias_own[h % 2]
+
+        def join(r, block, lse):
+            wait(side_in.at[h, r], so_r.at[h, r])
+            wait(side_stat_in.at[h, r], st_r.at[h, r])
+            lse_side = columns_of(side_stat_in[h, r])[:, :1]
+            best = jnp.maximum(lse, lse_side)
+            share, share_side = jnp.exp2(lse - best), jnp.exp2(lse_side - best)
+            total = share + share_side
+            block = (block * share + side_in[h, r].astype(F32) * share_side) / total
+            return block.astype(BF16), as_row(best + jnp.log2(total), 256)
+
+        score_tile(0)
+        for i, (r, _) in enumerate(tiles):
+            if i < 7:
+                score_tile(i + 1)
+            if i == 4 and h < 2:
+                pass_queries(h + 1)
+            block, lse = weigh(held[i % 2], kv[h, 1].reshape(1024, 128))
+            if i < 4:
+                side_out[h, r], side_stat_out[h, r] = block.astype(BF16), as_row(lse, 256)
+                send(side_out.at[h, r], side_in.at[h, r], so_s.at[h], so_r.at[h, r], sibling)
+                send(side_stat_out.at[h, r], side_stat_in.at[h, r], st_s.at[h], st_r.at[h, r], sibling)
+            elif r:
+                part_out[h, r - 1], stat_out[h, r - 1] = join(r, block, lse)
+                send(part_out.at[h, r - 1], part_in.at[h, 4 - r], o_s.at[h], o_r.at[h], query_peer(h, r))
+                send(stat_out.at[h, r - 1], stat_in.at[h, 4 - r], t_s.at[h], t_r.at[h], query_peer(h, r))
+            else:
+                part_in[h, 0], stat_in[h, 0] = join(r, block, lse)
 
     def merge(h):
-        wait(part_in.at[h, pl.ds(1, 7)], o_r.at[h])
-        wait(stat_in.at[h, pl.ds(1, 7)], t_r.at[h])
-        pairs = [jnp.where(lanes < 64, own_stat_in[2 * i, h : h + 1, :], jnp.roll(own_stat_in[2 * i + 1, h : h + 1, :], 64, axis=1)) for i in range(2)]
+        wait(part_in.at[h, pl.ds(1, 3)], o_r.at[h])
+        wait(stat_in.at[h, pl.ds(1, 3)], t_r.at[h])
+        first = lanes[:1] < 64
+        pairs = [jnp.where(first, own_stat_in[2 * i, h : h + 1, :], jnp.roll(own_stat_in[2 * i + 1, h : h + 1, :], 64, axis=1)) for i in range(2)]
         stats = jnp.concatenate([stat_in[h, :, 0, :], jnp.concatenate(pairs, axis=1)], axis=0)
         shares = jnp.exp2(stats - jnp.max(stats, axis=0, keepdims=True))
         share_cols = columns_of(shares / jnp.sum(shares, axis=0, keepdims=True))
-        summed = own_in[h].reshape(256, 128).astype(F32) * share_cols[:, 8:9]
-        for i in range(8):
+        summed = own_in[h].reshape(256, 128).astype(F32) * share_cols[:, 4:5]
+        for i in range(4):
             summed = summed + part_in[h, i].astype(F32) * share_cols[:, i : i + 1]
         block = summed.astype(BF16)
         merged[h, 16:272] = block
@@ -268,14 +304,12 @@
             send(window(to_z), dst, b_s.at[h], b_r.at[h], device(x, y, to_z, c))
 
     attend_far(0)
-    pass_queries(1)
     attend_home()
     attend_far(1)
-    pass_queries(2)
+    attend_far(2)
     wait(own_in, own_r.at[0])
     wait(own_stat_in, ot_r.at[0])
     merge(0)
-    attend_far(2)
     merge(1)
     merge(2)
 
@@ -314,8 +348,10 @@
         wait(q.at[h, 0, pl.ds(1, 3)], xq_s.at[h])
         wait(q.at[h, 0], qf_s.at[h])
         wait(kv.at[h, :, pl.ds(0, 3)], yk_s.at[h])
-        wait(part_out.at[h, pl.ds(0, 7)], o_s.at[h])
-        wait(stat_out.at[h, pl.ds(0, 7)], t_s.at[h])
+        wait(part_out.at[h], o_s.at[h])
+        wait(stat_out.at[h], t_s.at[h])
+        wait(side_out.at[h], so_s.at[h])
+        wait(side_stat_out.at[h], st_s.at[h])
         wait(merged.at[h, pl.ds(0, 192)], b_s.at[h])
 
         @pl.when(step_here == 1)
@@ -359,21 +395,24 @@
     sems = {
         "zq_s": (3,), "zq_r": (3,), "zk_s": (3,), "zs_s": (3,), "zk_r": (3,), "home_s": (1,), "home_r": (1,),
         "w_s": (1,), "w_r": (1,), "w_l": (1,), "xq_s": (3,), "xq_r": (3,), "qf_s": (3,), "qf_r": (3,),
-        "yk_s": (3,), "yk_r": (3, 3), "o_s": (3,), "o_r": (3,), "t_s": (3,), "t_r": (3,), "b_s": (3,), "b_r": (3,),
+        "yk_s": (3,), "yk_r": (3, 3), "so_s": (3,), "so_r": (3, 4), "st_s": (3,), "st_r": (3, 4), "o_s": (3,), "o_r": (3,), "t_s": (3,), "t_r": (3,), "b_s": (3,), "b_r": (3,),
         "own_s": (1,), "own_r": (1,), "ot_s": (1,), "ot_r": (1,), "p_s": (4,), "p_r": (4,),
-        "i_l": (3,),
+        "i_l": (4,),
     }
     buffers = {
-        "inputs": ((2, 32, 3072), BF16), "gate": ((2, 3072), F32), "stale_raw": ((128, 2, 384), BF16),
+        "inputs": ((2, 32, 3072), BF16), "gate": ((2, 3072), F32), "fresh": ((2, 3, 32, 1536), BF16),
+        "stale_raw": ((128, 2, 384), BF16),
         "stale": ((2, 2, 2, 32, 384), BF16),
         "q": ((3, 2, 4, 8, 32, 128), BF16), "kv": ((3, 2, 4, 8, 32, 128), BF16),
-        "part_out": ((3, 7, 256, 128), BF16), "part_in": ((3, 8, 256, 128), BF16),
-        "stat_out": ((3, 7, 8, 256), F32), "stat_in": ((3, 8, 8, 256), F32),
+        "side_out": ((3, 4, 256, 128), BF16), "side_in": ((3, 4, 256, 128), BF16),
+        "side_stat_out": ((3, 4, 8, 256), F32), "side_stat_in": ((3, 4, 8, 256), F32),
+        "part_out": ((3, 3, 256, 128), BF16), "part_in": ((3, 4, 256, 128), BF16),
+        "stat_out": ((3, 3, 8, 256), F32), "stat_in": ((3, 4, 8, 256), F32),
         "merged": ((3, 288, 128), BF16), "att": ((2, 2, 3, 64, 128), BF16),
         "home": ((2, 3, 2, 2, 32, 384), BF16), "own_out": ((2, 2, 3, 64, 128), BF16), "own_in": ((3, 4, 64, 128), BF16),
         "own_stat_out": ((2, 2, 8, 128), F32), "own_stat_in": ((4, 8, 128), F32), "w_all": ((2, 384, 3072), BF16),
         "near_out": ((4, 2, 2, 16, 768), BF16), "near_in": ((4, 2, 2, 16, 768), BF16), "kept": ((4, 64, 768), F32),
-        "bias_own": ((256, 1024), F32),
+        "bias_own": ((2, 256, 1024), F32), "held": ((2, 256, 1024), F32),
     }
     call = pl.pallas_call(
         kernel,

time: 66.4 us -> 64.2 us (0.967); the launches traced: 66.2 us -> 63.3 us
  Pallas kernels: 64.5 us -> 61.5 us
    pallas_call x1, Pallas kernels: 64.5 us -> 61.5 us  [shards(): call(fresh, stale_kv, text_mask.reshape(2, 128), out_weight, inputs, gate)]
where the time goes in v3:
time: 64.2 us; the launch traced here: 63.3 us
  Pallas kernels  61.5 us (96%)
  local copies, waits for them, and re-layouts  1.77 us (3%)
    pallas_call x1, Pallas kernels, shards(): call(fresh, stale_kv, text_mask.reshape(2, 128), out_weight, inputs, gate)  61.5 us
    unnamed x1, local copies, waits for them, and re-layouts  1.77 us

profile of v3, /device:TPU:1, one launch (start us, length us, event | category | flops | bytes accessed | tf_op | source)
XLA Modules:
  0.0 63.3 jit_solution(8594065289258029403)
XLA Ops:
  0.0 61.5 %stale_patch_attention.1 = bf16[2,32,3072]{2,1,0:T(8,128)(2,1)} custom-call(bf16[2,3,32,1536]{3,2,1,0:T(8,128)(2,1)} %bitcast.2, bf16[128,2,384]{2,1,0:T(2,128)(2,1)} %stale_far.1, s32[2,128]{1,0:T(2,128)} %bitcast.3, bf16[384,3072]{1,0:T(8,128)(2,1)} %weight.1, bf16[2,32,3072]{2,1,0:T(8,128)(2,1)} %inputs_far.1, f32[2,3072]{1,0:T(2,128)} %gate_far.1), custom_call_target="tpu_custom_call" | custom-call | tf_op jit(solution)/shard_map/stale_patch_attention/pallas_call | solution.py:426
  61.6 1.8 %copy.8 = bf16[2,32,3072]{2,1,0:T(8,128)(2,1)} copy(bf16[2,32,3072]{2,1,0:T(8,128)(2,1)} %stale_patch_attention.1) | data formatting | bytes 786432

commit v4 on v3

--- a/solution.py
+++ b/solution.py
@@ -47,9 +47,9 @@
 
 def kernel(
     fresh_far, stale_far, mask, weight, inputs_far, gate_far, out,
-    inputs, gate, fresh, stale_raw, stale, q, kv, side_out, side_in, side_stat_out, side_stat_in, part_out, part_in, stat_out, stat_in, merged, att,
+    inputs, gate, fresh, stale_raw, stale, q, kv, part_out, part_in, stat_out, stat_in, merged, att,
     home, own_out, own_in, own_stat_out, own_stat_in, w_all, near_out, near_in, kept, bias_own, held,
-    zq_s, zq_r, zk_s, zs_s, zk_r, home_s, home_r, w_s, w_r, w_l, xq_s, xq_r, qf_s, qf_r, yk_s, yk_r, so_s, so_r, st_s, st_r,
+    zq_s, zq_r, zk_s, zs_s, zk_r, home_s, home_r, w_s, w_r, w_l, xq_s, xq_r, qf_s, qf_r, yk_s, yk_r,
     o_s, o_r, t_s, t_r, b_s, b_r, own_s, own_r, ot_s, ot_r, p_s, p_r, i_l,
 ):
     patch, head = lax.axis_index("patch"), lax.axis_index("head")
@@ -85,20 +85,21 @@
 
     @pl.loop(1, 4)
     def _(d):
-        greet(device((x + d) % 4, y, z, c))
-        greet(device(x, (y + d) % 4, z, c))
+        for lane in range(2):
+            greet(device((x + d) % 4, y, z, lane))
+            greet(device(x, (y + d) % 4, z, lane))
 
     to_stale.wait()
     to_fresh.wait()
     for kind in range(2):
         stale[kind] = stale_raw[:, kind, :].reshape(2, 2, 32, 384)
-    pl.semaphore_wait(barrier, 21)
-
-    def query_peer(h, d):
-        return device(x, (y + d) % 4, z, c) if h == 1 else device((x + d) % 4, y, z, c)
+    pl.semaphore_wait(barrier, 27)
+
+    def query_peer(h, d, lane):
+        return device(x, (y + d) % 4, z, lane) if h == 1 else device((x + d) % 4, y, z, lane)
 
     def key_peer(h, d):
-        return query_peer(1 - h % 2, d)
+        return query_peer(1 - h % 2, d, c)
 
     def key_slot(h):
         return x if h == 1 else y
@@ -190,7 +191,7 @@
 
         @pl.loop(1, 4)
         def _(d):
-            send(q.at[h, c, 0], q.at[h, c, 4 - d], xq_s.at[h], xq_r.at[h], query_peer(h, d))
+            send(q.at[h, c, 0], q.at[h, c, 4 - d], xq_s.at[h], xq_r.at[h], query_peer(h, d, c))
 
     gather(0)
     gather(1)
@@ -241,51 +242,41 @@
             wait(kv.at[h, :, (key_slot(h) + 4 - d) % 4], yk_r.at[h, d - 1])
         wait(q.at[h, 1 - c], qf_r.at[h])
 
-        tiles = [(r, lane) for lane in (1 - c, c) for r in (1, 2, 3, 0)]
+        tiles = [(r, c if same else 1 - c, same) for r in (2, 1, 3) for same in (True, False)]
+        tiles += [(0, 1 - c, False), (0, c, True)]
 
         def score_tile(i):
-            r, lane = tiles[i]
+            r, lane, _ = tiles[i]
             scores = score(q[h, lane, r].reshape(256, 128), kv[h, 0].reshape(1024, 128))
             held[i % 2] = far_bias(h, scores) if r else scores + bias_own[h % 2]
 
-        def join(r, block, lse):
-            wait(side_in.at[h, r], so_r.at[h, r])
-            wait(side_stat_in.at[h, r], st_r.at[h, r])
-            lse_side = columns_of(side_stat_in[h, r])[:, :1]
-            best = jnp.maximum(lse, lse_side)
-            share, share_side = jnp.exp2(lse - best), jnp.exp2(lse_side - best)
-            total = share + share_side
-            block = (block * share + side_in[h, r].astype(F32) * share_side) / total
-            return block.astype(BF16), as_row(best + jnp.log2(total), 256)
-
         score_tile(0)
-        for i, (r, _) in enumerate(tiles):
+        for i, (r, lane, same) in enumerate(tiles):
             if i < 7:
                 score_tile(i + 1)
             if i == 4 and h < 2:
                 pass_queries(h + 1)
             block, lse = weigh(held[i % 2], kv[h, 1].reshape(1024, 128))
-            if i < 4:
-                side_out[h, r], side_stat_out[h, r] = block.astype(BF16), as_row(lse, 256)
-                send(side_out.at[h, r], side_in.at[h, r], so_s.at[h], so_r.at[h, r], sibling)
-                send(side_stat_out.at[h, r], side_stat_in.at[h, r], st_s.at[h], st_r.at[h, r], sibling)
-            elif r:
-                part_out[h, r - 1], stat_out[h, r - 1] = join(r, block, lse)
-                send(part_out.at[h, r - 1], part_in.at[h, 4 - r], o_s.at[h], o_r.at[h], query_peer(h, r))
-                send(stat_out.at[h, r - 1], stat_in.at[h, 4 - r], t_s.at[h], t_r.at[h], query_peer(h, r))
+            block, lse = block.astype(BF16), as_row(lse, 256)
+            if i == 7:
+                part_in[h, 0], stat_in[h, 0] = block, lse
             else:
-                part_in[h, 0], stat_in[h, 0] = join(r, block, lse)
+                part_out[h, i], stat_out[h, i] = block, lse
+                slot = (4 - r) % 4 * 2 + (0 if same else 1)
+                to = query_peer(h, r, lane) if r else sibling
+                send(part_out.at[h, i], part_in.at[h, slot], o_s.at[h], o_r.at[h], to)
+                send(stat_out.at[h, i], stat_in.at[h, slot], t_s.at[h], t_r.at[h], to)
 
     def merge(h):
-        wait(part_in.at[h, pl.ds(1, 3)], o_r.at[h])
-        wait(stat_in.at[h, pl.ds(1, 3)], t_r.at[h])
+        wait(part_in.at[h, pl.ds(1, 7)], o_r.at[h])
+        wait(stat_in.at[h, pl.ds(1, 7)], t_r.at[h])
         first = lanes[:1] < 64
         pairs = [jnp.where(first, own_stat_in[2 * i, h : h + 1, :], jnp.roll(own_stat_in[2 * i + 1, h : h + 1, :], 64, axis=1)) for i in range(2)]
         stats = jnp.concatenate([stat_in[h, :, 0, :], jnp.concatenate(pairs, axis=1)], axis=0)
         shares = jnp.exp2(stats - jnp.max(stats, axis=0, keepdims=True))
         share_cols = columns_of(shares / jnp.sum(shares, axis=0, keepdims=True))
-        summed = own_in[h].reshape(256, 128).astype(F32) * share_cols[:, 4:5]
-        for i in range(4):
+        summed = own_in[h].reshape(256, 128).astype(F32) * share_cols[:, 8:9]
+        for i in range(8):
             summed = summed + part_in[h, i].astype(F32) * share_cols[:, i : i + 1]
         block = summed.astype(BF16)
         merged[h, 16:272] = block
@@ -350,8 +341,6 @@
         wait(kv.at[h, :, pl.ds(0, 3)], yk_s.at[h])
         wait(part_out.at[h], o_s.at[h])
         wait(stat_out.at[h], t_s.at[h])
-        wait(side_out.at[h], so_s.at[h])
-        wait(side_stat_out.at[h], st_s.at[h])
         wait(merged.at[h, pl.ds(0, 192)], b_s.at[h])
 
         @pl.when(step_here == 1)
@@ -395,7 +384,7 @@
     sems = {
         "zq_s": (3,), "zq_r": (3,), "zk_s": (3,), "zs_s": (3,), "zk_r": (3,), "home_s": (1,), "home_r": (1,),
         "w_s": (1,), "w_r": (1,), "w_l": (1,), "xq_s": (3,), "xq_r": (3,), "qf_s": (3,), "qf_r": (3,),
-        "yk_s": (3,), "yk_r": (3, 3), "so_s": (3,), "so_r": (3, 4), "st_s": (3,), "st_r": (3, 4), "o_s": (3,), "o_r": (3,), "t_s": (3,), "t_r": (3,), "b_s": (3,), "b_r": (3,),
+        "yk_s": (3,), "yk_r": (3, 3), "o_s": (3,), "o_r": (3,), "t_s": (3,), "t_r": (3,), "b_s": (3,), "b_r": (3,),
         "own_s": (1,), "own_r": (1,), "ot_s": (1,), "ot_r": (1,), "p_s": (4,), "p_r": (4,),
         "i_l": (4,),
     }
@@ -404,10 +393,8 @@
         "stale_raw": ((128, 2, 384), BF16),
         "stale": ((2, 2, 2, 32, 384), BF16),
         "q": ((3, 2, 4, 8, 32, 128), BF16), "kv": ((3, 2, 4, 8, 32, 128), BF16),
-        "side_out": ((3, 4, 256, 128), BF16), "side_in": ((3, 4, 256, 128), BF16),
-        "side_stat_out": ((3, 4, 8, 256), F32), "side_stat_in": ((3, 4, 8, 256), F32),
-        "part_out": ((3, 3, 256, 128), BF16), "part_in": ((3, 4, 256, 128), BF16),
-        "stat_out": ((3, 3, 8, 256), F32), "stat_in": ((3, 4, 8, 256), F32),
+        "part_out": ((3, 7, 256, 128), BF16), "part_in": ((3, 8, 256, 128), BF16),
+        "stat_out": ((3, 7, 8, 256), F32), "stat_in": ((3, 8, 8, 256), F32),
         "merged": ((3, 288, 128), BF16), "att": ((2, 2, 3, 64, 128), BF16),
         "home": ((2, 3, 2, 2, 32, 384), BF16), "own_out": ((2, 2, 3, 64, 128), BF16), "own_in": ((3, 4, 64, 128), BF16),
         "own_stat_out": ((2, 2, 8, 128), F32), "own_stat_in": ((4, 8, 128), F32), "w_all": ((2, 384, 3072), BF16),

time: 64.2 us -> 62.1 us (0.967)
  Pallas kernels: 61.5 us -> 59.5 us
    pallas_call x1, Pallas kernels: 61.5 us -> 59.5 us  [shards(): call(fresh, stale_kv, text_mask.reshape(2, 128), out_weight, inputs, gate)]
where the time goes in v4:
time: 62.1 us; the launch traced here: 61.3 us
  Pallas kernels  59.5 us (96%)
  local copies, waits for them, and re-layouts  1.77 us (3%)
    pallas_call x1, Pallas kernels, shards(): call(fresh, stale_kv, text_mask.reshape(2, 128), out_weight, inputs, gate)  59.5 us
    unnamed x1, local copies, waits for them, and re-layouts  1.77 us

profile of v4, /device:TPU:1, one launch (start us, length us, event | category | flops | bytes accessed | tf_op | source)
XLA Modules:
  0.0 61.3 jit_solution(13528176445336148991)
XLA Ops:
  0.0 59.5 %stale_patch_attention.1 = bf16[2,32,3072]{2,1,0:T(8,128)(2,1)} custom-call(bf16[2,3,32,1536]{3,2,1,0:T(8,128)(2,1)} %bitcast.2, bf16[128,2,384]{2,1,0:T(2,128)(2,1)} %stale_far.1, s32[2,128]{1,0:T(2,128)} %bitcast.3, bf16[384,3072]{1,0:T(8,128)(2,1)} %weight.1, bf16[2,32,3072]{2,1,0:T(8,128)(2,1)} %inputs_far.1, f32[2,3072]{1,0:T(2,128)} %gate_far.1), custom_call_target="tpu_custom_call" | custom-call | tf_op jit(solution)/shard_map/stale_patch_attention/pallas_call | solution.py:413
  59.5 1.8 %copy.8 = bf16[2,32,3072]{2,1,0:T(8,128)(2,1)} copy(bf16[2,32,3072]{2,1,0:T(8,128)(2,1)} %stale_patch_attention.1) | data formatting | bytes 786432
